TPU v7x, 512 devices: a whole 4x8x8 slice. The times are simulated.
512 devices in a mesh: patch: 64 (over z, y_lo, core), head: 8 (over y_hi, x).
Axes of the slice: x: 4, y: 8 (y_hi: 2, y_lo: 4; y = y_hi * 4 + y_lo), z: 8, core: 2. Of those that a mesh axis runs over, the one named last changes fastest.
Arguments:
- fresh: bfloat16 [3, 4, 1024, 3072], P(None, None, 'patch', 'head'), may hold values from -18 to 18
- still_masked: int32 [4, 1024], P(None, 'patch'), may hold values 0 or 1
- actions: int32 [4], replicated, may hold values from 0 to 7
- action_table: bfloat16 [8, 3, 3072], P(None, None, 'head'), may hold values from -3 to 3
- mask_vector: bfloat16 [3, 3072], P(None, 'head'), may hold values from -4 to 4
- position: bfloat16 [3, 1024, 3072], P(None, 'patch', 'head'), may hold values from -4 to 4
- cache: bfloat16 [2, 16, 4, 1024, 3072], P(None, None, None, 'patch', 'head'), may hold values from -18 to 18
- w_out: bfloat16 [3072, 5120], P('head', 'patch'), may hold values from -0.109375 to 0.109375
Outputs:
- update: float32 [4, 1024, 5120], P(None, 'patch', 'head')
All inputs are finite; a program needn't handle non-finite values. No bound on the sum of `still_masked` on one device may be relied on, other than what follows from the above.
Results may differ from a plain program's by a relative error of at most 0.0082.
Values may be sent and summed in bfloat16 or wider, within the bound.
A program may use at most 64 MiB of HBM per device.

v0:
```python
import jax
import jax.numpy as jnp
from jax import lax
from jax.sharding import PartitionSpec as P

HD = 128
NACT = 8


def split_heads(x):
    return x.reshape(x.shape[:-1] + (x.shape[-1] // HD, HD))


def shards(fresh, still_masked, actions, action_table, mask_vector, position, cache, w_out):
    onehot = (actions[:, None] == jnp.arange(NACT, dtype=jnp.int32)[None, :]).astype(jnp.float32)
    bias = jnp.einsum("ra,ach->crh", onehot, action_table.astype(jnp.float32))
    base = jnp.where(
        still_masked[None, :, :, None] == 1,
        mask_vector.astype(jnp.float32)[:, None, None, :],
        fresh.astype(jnp.float32),
    )
    embed = (base + bias[:, :, None, :] + position.astype(jnp.float32)[:, None, :, :]).astype(
        jnp.bfloat16
    )
    scale = HD ** (-0.5)
    query = split_heads(embed[0])
    own_key = split_heads(embed[1])
    own_value = split_heads(embed[2])
    keys_all, values_all = (
        lax.all_gather(embed[1], "patch", axis=1, tiled=True),
        lax.all_gather(embed[2], "patch", axis=1, tiled=True),
    )
    scores = (
        jnp.einsum(
            "rphd,rkhd->rhpk", query, split_heads(keys_all), preferred_element_type=jnp.float32
        )
        * scale
    )
    peak = jnp.max(scores, axis=-1, keepdims=True)
    expo = jnp.exp(scores - peak)
    total = jnp.sum(expo, axis=-1)
    summed = jnp.einsum(
        "rhpk,rkhd->rhpd",
        expo.astype(jnp.bfloat16),
        split_heads(values_all),
        preferred_element_type=jnp.float32,
    )
    spatial = summed / total[..., None]
    spatial = jnp.transpose(spatial, (0, 2, 1, 3))
    cache_key = split_heads(cache[0])
    cache_value = split_heads(cache[1])
    tscores = (
        jnp.einsum("rphd,frphd->frph", query, cache_key, preferred_element_type=jnp.float32) * scale
    )
    own = jnp.sum(query.astype(jnp.float32) * own_key.astype(jnp.float32), axis=-1) * scale
    tpeak = jnp.maximum(jnp.max(tscores, axis=0), own)
    texpo = jnp.exp(tscores - tpeak[None])
    oexpo = jnp.exp(own - tpeak)
    ttotal = jnp.sum(texpo, axis=0) + oexpo
    own_weight = oexpo.astype(jnp.bfloat16).astype(jnp.float32)
    temporal = jnp.einsum(
        "frph,frphd->rphd",
        texpo.astype(jnp.bfloat16),
        cache_value,
        preferred_element_type=jnp.float32,
    )
    temporal = (temporal + own_weight[..., None] * own_value.astype(jnp.float32)) / ttotal[
        ..., None
    ]
    attended = (spatial + temporal).reshape(embed.shape[1:]).astype(jnp.bfloat16)
    partial_value = jnp.einsum(
        "rph,hc->rpc",
        attended,
        lax.all_gather(w_out, "patch", axis=1, tiled=True),
        preferred_element_type=jnp.float32,
    )
    return lax.psum_scatter(partial_value, "head", scatter_dimension=2, tiled=True)


def solution(mesh):
    placed = (
        P(None, None, "patch", "head"),
        P(None, "patch"),
        P(),
        P(None, None, "head"),
        P(None, "head"),
        P(None, "patch", "head"),
        P(None, None, None, "patch", "head"),
        P("head", "patch"),
    )
    return jax.shard_map(
        shards, mesh=mesh, in_specs=placed, out_specs=P(None, "patch", "head"), check_vma=False
    )
```

profile of v0, /device:TPU:1, one launch (start us, length us, event | category | flops | bytes accessed | tf_op | source)
XLA Modules:
  0.0 477.2 jit_solution(7724439753330860788)
XLA Ops:
  6.5 0.9 convert_element_type.65
  7.4 0.7 convert_element_type.63
  8.1 0.7 broadcast_compare_fusion
  8.8 0.8 convolution_bitcast_fusion.1
  9.7 1.0 add_convert_fusion
  10.7 0.6 copy.54
  11.4 0.6 copy.58
  12.2 0.7 all-gather.6.cloned.1.call-update
  13.0 0.7 reshape.58
  14.1 0.3 reshape_squeeze.12
  14.4 0.2 copy-done.2
  14.6 0.7 fusion.8
  15.6 0.3 reshape_squeeze.13
  16.0 0.7 fusion.6
  16.7 119.3 %all-gather.8.cloned.1.call-done = bf16[1,4,1024,384]{3,1,0,2:T(4,128)(2,1)} async-done(((bf16[1,4,16,384]{3,1,0,2:T(4,128)(2,1)}), bf16[1,4,1024,384]{3,1,0,2:T(4,128)(2,1)}) %all-gather.8.cloned.1.call-update) | async-done | bytes 3145744 | tf_op jit(solution)/shard_map/all_gather | solution.py:30
  136.0 6.0 %copy.55 = bf16[1,4,1024,384]{2,3,1,0:T(8,128)(2,1)} copy(bf16[1,4,1024,384]{3,1,0,2:T(4,128)(2,1)} %all-gather.8.cloned.1.call-done) | data formatting | bytes 6291456 | tf_op jit(solution)/shard_map/all_gather | solution.py:30
  142.0 113.8 %all-gather.10.cloned.1.call-done = bf16[1,4,1024,384]{3,1,0,2:T(4,128)(2,1)} async-done(((bf16[1,4,16,384]{3,1,0,2:T(4,128)(2,1)}), bf16[1,4,1024,384]{3,1,0,2:T(4,128)(2,1)}) %all-gather.10.cloned.1.call-update) | async-done | bytes 3145744 | tf_op jit(solution)/shard_map/all_gather | solution.py:31
  255.8 4.3 copy.59
  260.2 2.5 fusion.27
  262.7 0.3 fusion.10
  262.9 1.0 fusion.5
  263.9 112.3 %all-gather.6.cloned.1.call-done = bf16[384,5120]{0,1:T(8,128)(2,1)} async-done(((bf16[384,80]{0,1:T(8,128)(2,1)}), bf16[384,5120]{0,1:T(8,128)(2,1)}) %all-gather.6.cloned.1.call-update) | async-done | bytes 3932176 | tf_op jit(solution)/shard_map/all_gather | solution.py:74
  376.2 4.5 fusion
  380.8 89.9 %reduce-scatter.2.cloned.1.call-done = f32[4,16,640]{2,1,0:T(8,128)} async-done(((f32[4,16,5120]{2,1,0:T(8,128)}), f32[4,16,640]{2,1,0:T(8,128)}) %reduce-scatter.2.cloned.1.call-update) | async-done | bytes 163856 | tf_op jit(solution)/shard_map/reduce_scatter | solution.py:77
  (25 shorter events, 1.1 us)
Async XLA Ops:
  6.5 2.3 copy-start
  6.5 7.4 %copy-start.1 = (bf16[2,16,4,16,384]{4,3,2,1,0:T(8,128)(2,1)S(1)}, bf16[2,16,4,16,384]{4,3,2,1,0:T(8,128)(2,1)}, u32[]{:S(2)}) copy-start(bf16[2,16,4,16,384]{4,3,2,1,0:T(8,128)(2,1)} %param.14) | copy-start | bytes 4718596
  6.5 129.5 %all-gather.8.cloned.1.call-start = ((), (), s32[]{:S(2)}) async-start(), calls=%async_computation.3 | async-start | bytes 3194880 | tf_op jit(solution)/shard_map/all_gather | solution.py:30
  11.4 244.4 %all-gather.10.cloned.1.call-start = ((), (), s32[]{:S(2)}) async-start(), calls=%async_computation.4 | async-start | bytes 3194880 | tf_op jit(solution)/shard_map/all_gather | solution.py:31
  12.1 364.1 %all-gather.6.cloned.1.call-start = ((), (), s32[]{:S(2)}) async-start(), calls=%async_computation.1 | async-start | bytes 3993600 | tf_op jit(solution)/shard_map/all_gather | solution.py:74
  12.9 457.8 %reduce-scatter.2.cloned.1.call-start = ((), (), s32[]{:S(2)}) async-start(), calls=%async_computation.2 | async-start | bytes 1474560 | tf_op jit(solution)/shard_map/reduce_scatter | solution.py:77
  13.7 0.9 copy-start.2
Sparse Core Ops, SparseCore 0:
  11.5 124.4 all-gather.7
  138.2 117.5 all-gather.9
  258.0 118.1 all-gather.5
  380.9 89.7 reduce-scatter.1
where the time goes:
time: 478 us; the launch traced here: 477 us
  waiting for transfers between devices  436 us (91%)
  local copies, waits for them, and re-layouts  13.5 us (3%)
  between operations  13.2 us (3%)
  matrix products  10.4 us (2%)
    all_gather x1, waiting for transfers between devices, shards(): lax.all_gather(embed[1], 'patch', axis=1, tiled=True)  119 us
    all_gather x1, waiting for transfers between devices, shards(): lax.all_gather(embed[2], 'patch', axis=1, tiled=True)  114 us
    all_gather x1, waiting for transfers between devices, shards(): lax.all_gather(w_out, 'patch', axis=1, tiled=True)  112 us
    reduce_scatter x1, waiting for transfers between devices, shards(): lax.psum_scatter(partial_value, 'head', scatter_dimension=2, tiled=True)  89.9 us
  transfers between devices with their start and end apart: 4, of which 4 were waited for; matrix products, arithmetic and copies ran while one was open for 4% of the time, Pallas kernels for 0%

commit v1 on v0

v1 whole, which is shorter than its diff:
```python
import functools

import jax
import jax.numpy as jnp
from jax import lax
from jax.experimental import pallas as pl
from jax.experimental.pallas import tpu as pltpu
from jax.sharding import PartitionSpec as P

HD = 128
NACT = 8
ROLL = 4
FRAMES = 16
SCALE = HD ** (-0.5)
LOG2E = 1.4426950408889634
PLACE = (0, 3, 5)
ZROWS, YROWS = 48, 32
NROWS = ZROWS + YROWS

BF16, F32 = jnp.bfloat16, jnp.float32


def nt_dot(a, b):
    return lax.dot_general(a, b, (((1,), (1,)), ((), ())), preferred_element_type=F32)


def kernel(
    actions, still_ref, table_ref, maskv_ref, fresh_hbm, pos_hbm, cache_hbm, w_hbm, out_ref,
    fresh, pos, cache, w_own, emb, qkv, kv_peer, o_buf, spat, temp, zg, yg, b_buf,
    cx_send, cx_own, cx_recv, y_send, y_recv,
    in_sem, qkv_sem, kv_sem, o_sem, t_sem, zg_sem, yg_sem, b_sem, bc_sem, cx_sem, y_sem,
    qkv_out, kv_out, o_out, t_out, zg_out, yg_out, bz_out, by_out, bc_out, cx_out, y_out,
):
    patch, head = lax.axis_index("patch"), lax.axis_index("head")
    z, yl, c = patch // 8, (patch // 2) % 4, patch % 2
    yh, x = head // 4, head % 4
    half = (z + yl) % 2
    base = (z // 2) * 2

    def at(z_=None, yl_=None, c_=None, yh_=None, x_=None):
        z_, yl_ = z if z_ is None else z_, yl if yl_ is None else yl_
        c_, yh_ = c if c_ is None else c_, yh if yh_ is None else yh_
        x_ = x if x_ is None else x_
        return {"patch": z_ * 8 + yl_ * 2 + c_, "head": yh_ * 4 + x_}

    def remote(src, dst, send, recv, device):
        return pltpu.make_async_remote_copy(
            src_ref=src, dst_ref=dst, send_sem=send, recv_sem=recv,
            device_id=device, device_id_type=pl.DeviceIdType.MESH,
        )

    def await_bytes(ref, sem):
        pltpu.make_async_copy(ref, ref, sem).wait()

    barrier = pltpu.get_barrier_semaphore()

    def hail(device):
        pl.semaphore_signal(barrier, inc=1, device_id=device, device_id_type=pl.DeviceIdType.MESH)

    def hail_group(i, carry):
        s = (z * 4 + yl + i) % 32
        hail(at(z_=s // 4, yl_=s % 4))
        return carry

    lax.fori_loop(1, 32, hail_group, 0)
    hail(at(c_=1 - c))
    for k in (1, 2, 3):
        hail(at(x_=(x + k) % 4))
    hail(at(yh_=1 - yh))
    hail(at(yh_=1 - yh, z_=base + 1 - z % 2))

    loads = [
        pltpu.make_async_copy(src, dst, in_sem.at[i])
        for i, (src, dst) in enumerate(
            ((fresh_hbm, fresh), (pos_hbm, pos), (w_hbm, w_own), (cache_hbm, cache))
        )
    ]
    for load in loads:
        load.start()

    loads[0].wait()
    loads[1].wait()
    diagonal = lax.broadcasted_iota(jnp.int32, (16, 16), 0) == lax.broadcasted_iota(
        jnp.int32, (16, 16), 1
    )
    row_of = lax.broadcasted_iota(jnp.int32, (NACT, 384), 0)
    for r in range(ROLL):
        flags = jnp.broadcast_to(still_ref[r : r + 1, :], (16, 16))
        masked = jnp.sum(jnp.where(diagonal, flags, 0).astype(F32), axis=1, keepdims=True) > 0.5
        for i in range(3):
            bias = jnp.sum(
                jnp.where(row_of == actions[r], table_ref[i].astype(F32), 0.0), axis=0, keepdims=True
            )
            mask_row = maskv_ref[i : i + 1, :].astype(F32)
            start = jnp.where(masked, mask_row, fresh[i, r].astype(F32))
            whole = (start + bias + pos[i].astype(F32)).astype(BF16)
            for h in range(3):
                emb[r * 3 + h, i] = whole[:, h * HD : (h + 1) * HD]

    loads[3].wait()

    def temporal(r, carry):
        for h in range(3):
            lanes = slice(h * HD, (h + 1) * HD)
            q = emb[r * 3 + h, 0].astype(F32)
            own_k = emb[r * 3 + h, 1].astype(F32)
            own_v = emb[r * 3 + h, 2].astype(F32)
            keys = cache[0, :, r, :, lanes].astype(F32)
            s = jnp.sum(q[None] * keys, axis=-1, keepdims=True) * SCALE
            own = jnp.sum(q * own_k, axis=-1, keepdims=True) * SCALE
            peak = jnp.maximum(jnp.max(s, axis=0), own)
            e = jnp.exp(s - peak[None])
            own_e = jnp.exp(own - peak)
            total = jnp.sum(e, axis=0) + own_e
            weights = e.astype(BF16).astype(F32)
            values = cache[1, :, r, :, lanes].astype(F32)
            summed = jnp.sum(weights * values, axis=0)
            summed = summed + own_e.astype(BF16).astype(F32) * own_v
            temp[z % 2, r, :, lanes] = summed / total
        return carry

    lax.fori_loop(0, ROLL, temporal, 0)

    loads[2].wait()
    pl.semaphore_wait(barrier, 37)

    me = z * 4 + yl
    pair_head = jnp.int32(-1)
    for h in range(3):
        pair_head = jnp.where((2 * yl + PLACE[h]) % 8 == z, h, pair_head)
    attends = pair_head >= 0
    for r in range(ROLL):
        for h in range(3):
            zd = (2 * r + PLACE[h]) % 8
            here = jnp.logical_and(z == zd, yl == r)

            @pl.when(here)
            def _(r=r, h=h):
                pltpu.make_async_copy(emb.at[r * 3 + h], qkv.at[me], qkv_sem).start()

            @pl.when(jnp.logical_not(here))
            def _(r=r, h=h, zd=zd):
                remote(
                    emb.at[r * 3 + h], qkv.at[me], qkv_out, qkv_sem, at(z_=zd, yl_=r)
                ).start()

    pltpu.make_async_copy(w_own.at[pl.ds(ZROWS, YROWS)], yg.at[yl], yg_sem).start()
    for k in range(1, 4):
        remote(
            w_own.at[pl.ds(ZROWS, YROWS)], yg.at[yl], yg_out, yg_sem, at(yl_=(yl + k) % 4)
        ).start()
    pltpu.make_async_copy(w_own.at[pl.ds(0, ZROWS)], zg.at[z], zg_sem).start()
    for k in range(1, 8):
        remote(
            w_own.at[pl.ds(0, ZROWS)], zg.at[z], zg_out, zg_sem, at(z_=(z + k) % 8)
        ).start()
    remote(temp.at[z % 2], temp.at[z % 2], t_out, t_sem, at(z_=base + 1 - z % 2)).start()

    await_bytes(yg, yg_sem)
    first = (z // 4 + yl) % 2

    def spread_z(k, carry):
        zd = first + 2 * k

        @pl.when(zd == z)
        def _():
            pltpu.make_async_copy(
                yg, b_buf.at[z % 4, :, c, pl.ds(ZROWS, YROWS)], b_sem
            ).start()

        @pl.when(zd != z)
        def _():
            remote(
                yg, b_buf.at[z % 4, :, c, pl.ds(ZROWS, YROWS)], by_out, b_sem, at(z_=zd)
            ).start()

        return carry

    lax.fori_loop(0, 4, spread_z, 0)

    @pl.when(attends)
    def _():
        await_bytes(qkv, qkv_sem)
        remote(qkv.at[:, pl.ds(1, 2)], kv_peer, kv_out, kv_sem, at(c_=1 - c)).start()

    await_bytes(zg, zg_sem)
    pltpu.make_async_copy(
        zg.at[pl.ds(half * 4, 4)], b_buf.at[:, yl, c, pl.ds(0, ZROWS)], b_sem
    ).start()
    for k in range(1, 4):
        yd = (yl + k) % 4
        remote(
            zg.at[pl.ds(((z + yd) % 2) * 4, 4)],
            b_buf.at[:, yl, c, pl.ds(0, ZROWS)],
            bz_out, b_sem, at(yl_=yd),
        ).start()

    @pl.when(attends)
    def _():
        await_bytes(kv_peer, kv_sem)
        c2 = SCALE * LOG2E

        def attend(i, carry):
            q = qkv[pl.ds(i * 8, 8), 0].reshape(128, HD)
            s_a = nt_dot(q, qkv[:, 1].reshape(512, HD))
            s_b = nt_dot(q, kv_peer[:, 0].reshape(512, HD))
            peak = jnp.maximum(
                jnp.max(s_a, axis=-1, keepdims=True), jnp.max(s_b, axis=-1, keepdims=True)
            )
            e_a = jnp.exp2((s_a - peak) * c2)
            e_b = jnp.exp2((s_b - peak) * c2)
            total = jnp.sum(e_a, axis=-1, keepdims=True) + jnp.sum(e_b, axis=-1, keepdims=True)
            o = jnp.dot(
                e_a.astype(BF16), qkv[:, 2].reshape(512, HD), preferred_element_type=F32
            ) + jnp.dot(
                e_b.astype(BF16), kv_peer[:, 1].reshape(512, HD), preferred_element_type=F32
            )
            o_buf[i] = (o / total).astype(BF16).reshape(2, 4, 16, HD)
            for b in range(2):
                for yd in range(4):
                    zd = 2 * i + b
                    here = jnp.logical_and(zd == z, yl == yd)
                    src, dst = o_buf.at[i, :, yd], spat.at[pair_head, :, yl]

                    @pl.when(here)
                    def _(src=src, dst=dst):
                        pltpu.make_async_copy(src, dst, o_sem).start()

                    @pl.when(jnp.logical_not(here))
                    def _(src=src, dst=dst, zd=zd, yd=yd):
                        remote(src, dst, o_out, o_sem, at(z_=zd, yl_=yd)).start()

            return carry

        lax.fori_loop(0, 4, attend, 0)

    await_bytes(b_buf.at[:, :, c], b_sem)
    remote(b_buf.at[:, :, c], b_buf.at[:, :, c], bc_out, bc_sem, at(c_=1 - c)).start()

    await_bytes(temp.at[0], t_sem)
    await_bytes(spat, o_sem)
    attended = jnp.concatenate(
        [
            (
                spat[h].astype(F32).reshape(128, HD)
                + temp[:, :, :, h * HD : (h + 1) * HD].reshape(128, HD)
            ).astype(BF16)
            for h in range(3)
        ],
        axis=1,
    )
    await_bytes(b_buf.at[:, :, 1 - c], bc_sem)

    for n, k in enumerate((2, 1, 3)):
        xd = (x + k) % 4
        part = nt_dot(attended, b_buf[xd].reshape(640, 384))
        cx_send[n] = part.astype(BF16).reshape(2, 64, 640)
        remote(
            cx_send.at[n], cx_recv.at[n], cx_out, cx_sem, at(x_=xd)
        ).start()
    cx_own[...] = nt_dot(attended, b_buf[x].reshape(640, 384)).reshape(2, 64, 640)
    await_bytes(cx_recv, cx_sem)

    mine = yh == half

    def total_of(zz):
        return (
            cx_own[zz]
            + cx_recv[0, zz].astype(F32)
            + cx_recv[1, zz].astype(F32)
            + cx_recv[2, zz].astype(F32)
        )

    other = 1 - z % 2
    y_send[0] = total_of(other).astype(BF16)
    remote(
        y_send.at[0], y_recv.at[yh], y_out, y_sem, at(z_=base + other, yh_=half)
    ).start()

    @pl.when(mine)
    def _():
        kept = total_of(z % 2)
        await_bytes(y_recv.at[0], y_sem)
        out_ref[...] = (kept + y_recv[1 - yh].astype(F32)).reshape(4, 16, 640)
        await_bytes(y_send.at[0], y_out)

    @pl.when(jnp.logical_not(mine))
    def _():
        y_send[1] = total_of(z % 2).astype(BF16)
        remote(y_send.at[1], y_recv.at[yh], y_out, y_sem, at(yh_=half)).start()
        await_bytes(y_recv, y_sem)
        out_ref[...] = (y_recv[0].astype(F32) + y_recv[1].astype(F32)).reshape(4, 16, 640)
        await_bytes(y_send, y_out)

    @pl.when(attends)
    def _():
        await_bytes(emb.at[pl.ds(0, 11)], qkv_out)
        await_bytes(kv_peer, kv_out)
        await_bytes(kv_peer.at[pl.ds(0, 31)], o_out)

    @pl.when(jnp.logical_not(attends))
    def _():
        await_bytes(emb, qkv_out)

    await_bytes(yg.at[pl.ds(0, 3)], yg_out)
    await_bytes(zg.at[pl.ds(0, 7)], zg_out)
    await_bytes(temp.at[0], t_out)
    sends = z % 2 == first

    @pl.when(sends)
    def _():
        await_bytes(b_buf.at[pl.ds(0, 3), :, 0, pl.ds(0, YROWS)], by_out)

    @pl.when(jnp.logical_not(sends))
    def _():
        await_bytes(b_buf.at[:, :, 0, pl.ds(0, YROWS)], by_out)

    await_bytes(b_buf.at[:, pl.ds(0, 3), 0, pl.ds(0, ZROWS)], bz_out)
    await_bytes(b_buf.at[:, :, 0], bc_out)
    await_bytes(cx_send, cx_out)


def shards(fresh, still_masked, actions, action_table, mask_vector, position, cache, w_out):
    anywhere = pl.BlockSpec(memory_space=pl.ANY)
    vmem = pl.BlockSpec(memory_space=pltpu.VMEM)
    smem = pl.BlockSpec(memory_space=pltpu.SMEM)
    dma = pltpu.SemaphoreType.DMA
    return pl.pallas_call(
        kernel,
        out_shape=jax.ShapeDtypeStruct((4, 16, 640), F32),
        in_specs=[smem, vmem, vmem, vmem, anywhere, anywhere, anywhere, anywhere],
        out_specs=vmem,
        scratch_shapes=[
            pltpu.VMEM((3, 4, 16, 384), BF16),
            pltpu.VMEM((3, 16, 384), BF16),
            pltpu.VMEM((2, 16, 4, 16, 384), BF16),
            pltpu.VMEM((NROWS, 384), BF16),
            pltpu.VMEM((12, 3, 16, HD), BF16),
            pltpu.VMEM((32, 3, 16, HD), BF16),
            pltpu.VMEM((32, 2, 16, HD), BF16),
            pltpu.VMEM((4, 2, 4, 16, HD), BF16),
            pltpu.VMEM((3, 2, 4, 16, HD), BF16),
            pltpu.VMEM((2, 4, 16, 384), F32),
            pltpu.VMEM((8, ZROWS, 384), BF16),
            pltpu.VMEM((4, YROWS, 384), BF16),
            pltpu.VMEM((4, 4, 2, NROWS, 384), BF16),
            pltpu.VMEM((3, 2, 64, 640), BF16),
            pltpu.VMEM((2, 64, 640), F32),
            pltpu.VMEM((3, 2, 64, 640), BF16),
            pltpu.VMEM((2, 64, 640), BF16),
            pltpu.VMEM((2, 64, 640), BF16),
            dma((4,)),
        ]
        + [dma] * 21,
        compiler_params=pltpu.CompilerParams(
            collective_id=0, has_side_effects=True, vmem_limit_bytes=40 << 20
        ),
        cost_estimate=pl.CostEstimate(
            flops=400_000_000, bytes_accessed=2_000_000, transcendentals=600_000
        ),
    )(
        actions,
        still_masked,
        jnp.transpose(action_table, (1, 0, 2)),
        mask_vector,
        fresh,
        position,
        cache,
        jnp.transpose(w_out),
    )


def solution(mesh):
    placed = (
        P(None, None, "patch", "head"),
        P(None, "patch"),
        P(),
        P(None, None, "head"),
        P(None, "head"),
        P(None, "patch", "head"),
        P(None, None, None, "patch", "head"),
        P("head", "patch"),
    )
    return jax.shard_map(
        shards, mesh=mesh, in_specs=placed, out_specs=P(None, "patch", "head"), check_vma=False
    )
```

time: 478 us -> 75.1 us (0.16)
  the two profiles are of different devices: /device:TPU:1 before, /device:TPU:8 now
where the time goes in v1:
time: 75.1 us; the launch traced here: 74.7 us
  Pallas kernels  67.4 us (90%)
  local copies, waits for them, and re-layouts  7.32 us (10%)
    pallas_call x1, Pallas kernels, shards(): pl.pallas_call(kernel, out_shape=jax.ShapeDtypeStruct((4, 16, 640), F32),...  67.4 us
    unnamed x17, local copies, waits for them, and re-layouts  7.32 us

profile of v1, /device:TPU:8, one launch (start us, length us, event | category | flops | bytes accessed | tf_op | source)
XLA Modules:
  0.0 74.7 jit_solution(9523482140920724527)
XLA Ops:
  0.0 0.0 copy-start
  0.0 1.4 %copy-done = bf16[2,16,4,16,384]{4,3,2,1,0:T(8,128)(2,1)S(1)} copy-done((bf16[2,16,4,16,384]{4,3,2,1,0:T(8,128)(2,1)S(1)}, bf16[2,16,4,16,384]{4,3,2,1,0:T(8,128)(2,1)}, u32[]{:S(2)}) %copy-start) | copy-done | bytes 1572888
  1.4 0.0 copy-start.1
  1.4 0.9 %copy-done.1 = bf16[3,4,16,384]{3,2,1,0:T(8,128)(2,1)S(1)} copy-done((bf16[3,4,16,384]{3,2,1,0:T(8,128)(2,1)S(1)}, bf16[3,4,16,384]{3,2,1,0:T(8,128)(2,1)}, u32[]{:S(2)}) %copy-start.1) | copy-done | bytes 147480
  2.3 0.0 copy-start.2
  2.3 0.8 %copy-done.2 = bf16[384,80]{0,1:T(8,128)(2,1)S(1)} copy-done((bf16[384,80]{0,1:T(8,128)(2,1)S(1)}, bf16[384,80]{0,1:T(8,128)(2,1)}, u32[]{:S(2)}) %copy-start.2) | copy-done | bytes 61464
  3.1 0.0 copy-start.3
  3.2 0.8 %copy-done.3 = bf16[3,16,384]{2,1,0:T(8,128)(2,1)S(1)} copy-done((bf16[3,16,384]{2,1,0:T(8,128)(2,1)S(1)}, bf16[3,16,384]{2,1,0:T(8,128)(2,1)}, u32[]{:S(2)}) %copy-start.3) | copy-done | bytes 36888
  3.9 0.0 copy-start.4
  3.9 0.7 copy-done.4
  4.6 0.0 copy-start.5
  4.6 0.7 copy-done.5
  5.3 0.0 copy-start.6
  5.3 0.7 copy-done.6
  6.0 0.0 copy-start.7
  6.0 0.7 copy-done.7
  6.7 67.4 %shard_map.82 = f32[4,16,640]{2,1,0:T(8,128)S(1)} custom-call(s32[4]{0:T(128)S(1)} %copy-done.7, s32[4,16]{1,0:T(4,128)S(1)} %copy-done.6, bf16[3,8,384]{2,1,0:T(8,128)(2,1)S(1)} %bitcast.3, bf16[3,384]{1,0:T(4,128)(2,1)S(1)} %copy-done.5, bf16[3,4,16,384]{3,2,1,0:T(8,128)(2,1)S(1)} %copy-done.1, bf16[3,16,384]{2,1,0:T(8,128)(2,1)S(1)} %copy-done.3, ...), custom_call_target="tpu_custom_call" | custom-call | flops 400000000 | bytes 2000000 | tf_op jit(solution)/shard_map/pallas_call | solution.py:328
  74.0 0.7 copy.10
Async XLA Ops:
  0.0 1.4 %copy-start = (bf16[2,16,4,16,384]{4,3,2,1,0:T(8,128)(2,1)S(1)}, bf16[2,16,4,16,384]{4,3,2,1,0:T(8,128)(2,1)}, u32[]{:S(2)}) copy-start(bf16[2,16,4,16,384]{4,3,2,1,0:T(8,128)(2,1)} %cache_hbm.1) | copy-start | bytes 4718596
  1.4 0.9 %copy-start.1 = (bf16[3,4,16,384]{3,2,1,0:T(8,128)(2,1)S(1)}, bf16[3,4,16,384]{3,2,1,0:T(8,128)(2,1)}, u32[]{:S(2)}) copy-start(bf16[3,4,16,384]{3,2,1,0:T(8,128)(2,1)} %fresh_hbm.1) | copy-start | bytes 442372
  2.3 0.8 %copy-start.2 = (bf16[384,80]{0,1:T(8,128)(2,1)S(1)}, bf16[384,80]{0,1:T(8,128)(2,1)}, u32[]{:S(2)}) copy-start(bf16[384,80]{0,1:T(8,128)(2,1)} %param.15) | copy-start | bytes 184324
  3.1 0.8 %copy-start.3 = (bf16[3,16,384]{2,1,0:T(8,128)(2,1)S(1)}, bf16[3,16,384]{2,1,0:T(8,128)(2,1)}, u32[]{:S(2)}) copy-start(bf16[3,16,384]{2,1,0:T(8,128)(2,1)} %pos_hbm.1) | copy-start | bytes 110596
  3.9 0.7 copy-start.4
  4.6 0.7 copy-start.5
  5.3 0.7 copy-start.6
  6.0 0.7 copy-start.7

commit v2 on v1

v2 whole, which is shorter than its diff:
```python
import functools

import jax
import jax.numpy as jnp
from jax import lax
from jax.experimental import pallas as pl
from jax.experimental.pallas import tpu as pltpu
from jax.sharding import PartitionSpec as P

HD = 128
NACT = 8
ROLL = 4
FRAMES = 16
SCALE = HD ** (-0.5)
LOG2E = 1.4426950408889634
PLACE = (0, 3, 5)
ZROWS, YROWS = 32, 48
NROWS = ZROWS + YROWS

BF16, F32 = jnp.bfloat16, jnp.float32


def nt_dot(a, b):
    return lax.dot_general(a, b, (((1,), (1,)), ((), ())), preferred_element_type=F32)


def kernel(
    actions, still_ref, table_ref, maskv_ref, fresh_hbm, pos_hbm, cache_hbm, w_hbm, y_out_ref,
    fresh, pos, cache, w_own, emb, qkv, kv_peer, t_send, t_recv, o_buf, att, near, b_buf,
    cx_send, cx_own, cx_recv, y_send,
    in_sem, o_out, cx_sem, qkv_sem, kv_sem, o_sem, t_sem, near_sem, b_sem, bz_sem, by_sem,
    bc_sem, bd_sem, y_sem,
    qkv_out, kv_out, t_out, near_out, b_out, bz_out, by_out, bc_out, bd_out, cx_out, y_out,
):
    patch, head = lax.axis_index("patch"), lax.axis_index("head")
    z, yl, c = patch // 8, (patch // 2) % 4, patch % 2
    yh, x = head // 4, head % 4
    yy, yb = yl // 2, yl % 2
    half = (z + yy) % 2
    base = (z // 2) * 2

    def at(z_=None, yl_=None, c_=None, yh_=None, x_=None):
        z_, yl_ = z if z_ is None else z_, yl if yl_ is None else yl_
        c_, yh_ = c if c_ is None else c_, yh if yh_ is None else yh_
        x_ = x if x_ is None else x_
        return {"patch": z_ * 8 + yl_ * 2 + c_, "head": yh_ * 4 + x_}

    def remote(src, dst, send, recv, device):
        return pltpu.make_async_remote_copy(
            src_ref=src, dst_ref=dst, send_sem=send, recv_sem=recv,
            device_id=device, device_id_type=pl.DeviceIdType.MESH,
        )

    def await_bytes(ref, sem):
        pltpu.make_async_copy(ref, ref, sem).wait()

    loads = [
        pltpu.make_async_copy(src, dst, in_sem.at[i])
        for i, (src, dst) in enumerate(
            ((fresh_hbm, fresh), (pos_hbm, pos), (w_hbm, w_own), (cache_hbm, cache))
        )
    ]
    for load in loads:
        load.start()

    barrier = pltpu.get_barrier_semaphore()

    def hail(device):
        pl.semaphore_signal(barrier, inc=1, device_id=device, device_id_type=pl.DeviceIdType.MESH)

    def hail_group(i, carry):
        s = (z * 4 + yl + i) % 32
        hail(at(z_=s // 4, yl_=s % 4))
        return carry

    lax.fori_loop(1, 32, hail_group, 0)
    hail(at(c_=1 - c))
    for k in (1, 2, 3):
        hail(at(x_=(x + k) % 4))
    for zz in range(2):
        for w in range(2):
            hail(at(yh_=1 - yh, z_=base + zz, yl_=2 * w + yb))

    loads[0].wait()
    loads[1].wait()
    diagonal = lax.broadcasted_iota(jnp.int32, (16, 16), 0) == lax.broadcasted_iota(
        jnp.int32, (16, 16), 1
    )
    row_of = lax.broadcasted_iota(jnp.int32, (NACT, 384), 0)
    for r in range(ROLL):
        flags = jnp.broadcast_to(still_ref[r : r + 1, :], (16, 16))
        masked = jnp.sum(jnp.where(diagonal, flags, 0).astype(F32), axis=1, keepdims=True) > 0.5
        for i in range(3):
            bias = jnp.sum(
                jnp.where(row_of == actions[r], table_ref[i].astype(F32), 0.0), axis=0, keepdims=True
            )
            mask_row = maskv_ref[i : i + 1, :].astype(F32)
            start = jnp.where(masked, mask_row, fresh[i, r].astype(F32))
            whole = (start + bias + pos[i].astype(F32)).astype(BF16)
            for h in range(3):
                emb[r * 3 + h, i] = whole[:, h * HD : (h + 1) * HD]

    loads[2].wait()
    pl.semaphore_wait(barrier, 39)

    me = z * 4 + yl
    pair_head = jnp.int32(-1)
    for h in range(3):
        pair_head = jnp.where((2 * yl + PLACE[h]) % 8 == z, h, pair_head)
    attends = pair_head >= 0

    def to_attending(src, dst, send, recv, r, h):
        zd = (2 * r + PLACE[h]) % 8
        here = jnp.logical_and(z == zd, yl == r)

        @pl.when(here)
        def _():
            pltpu.make_async_copy(src, dst, recv).start()

        @pl.when(jnp.logical_not(here))
        def _():
            remote(src, dst, send, recv, at(z_=zd, yl_=r)).start()

    for r in range(ROLL):
        for h in range(3):
            to_attending(emb.at[r * 3 + h], qkv.at[me], qkv_out, qkv_sem, r, h)

    first = (z // 4 + yy) % 2
    own_rows = pl.multiple_of((yb * 2 + c) * NROWS, 16)
    near_rows = pl.multiple_of(((1 - yb) * 2 + c) * NROWS, 16)

    def spread(src, rows, size, send, recv):
        def one(k, carry):
            zd = first + 2 * k
            dst = b_buf.at[z % 4, pl.ds(rows, size)]

            @pl.when(zd == z)
            def _():
                pltpu.make_async_copy(src, dst, recv).start()

            @pl.when(zd != z)
            def _():
                remote(src, dst, send, recv, at(z_=zd)).start()

            return carry

        lax.fori_loop(0, 4, one, 0)

    remote(
        w_own.at[pl.ds(ZROWS, YROWS)], near, near_out, near_sem, at(yl_=2 * yy + 1 - yb)
    ).start()
    spread(w_own, own_rows, NROWS, b_out, b_sem)

    loads[3].wait()

    def temporal(r, carry):
        for h in range(3):
            lanes = slice(h * HD, (h + 1) * HD)
            q = emb[r * 3 + h, 0].astype(F32)
            own_k = emb[r * 3 + h, 1].astype(F32)
            own_v = emb[r * 3 + h, 2].astype(F32)
            keys = cache[0, :, r, :, lanes].astype(F32)
            s = jnp.sum(q[None] * keys, axis=-1, keepdims=True) * SCALE
            own = jnp.sum(q * own_k, axis=-1, keepdims=True) * SCALE
            peak = jnp.maximum(jnp.max(s, axis=0), own)
            e = jnp.exp(s - peak[None])
            own_e = jnp.exp(own - peak)
            total = jnp.sum(e, axis=0) + own_e
            weights = e.astype(BF16).astype(F32)
            values = cache[1, :, r, :, lanes].astype(F32)
            summed = jnp.sum(weights * values, axis=0)
            summed = summed + own_e.astype(BF16).astype(F32) * own_v
            t_send[r * 3 + h] = (summed / total).astype(BF16)
        return carry

    lax.fori_loop(0, ROLL, temporal, 0)

    for r in range(ROLL):
        for h in range(3):
            to_attending(t_send.at[r * 3 + h], t_recv.at[me], t_out, t_sem, r, h)

    await_bytes(near, near_sem)
    spread(near, near_rows + ZROWS, YROWS, bz_out, bz_sem)

    @pl.when(attends)
    def _():
        await_bytes(qkv, qkv_sem)
        remote(qkv.at[:, pl.ds(1, 2)], kv_peer, kv_out, kv_sem, at(c_=1 - c)).start()

    await_bytes(b_buf.at[:, pl.ds(own_rows, NROWS)], b_sem)
    went = b_buf.at[:, pl.ds(own_rows, ZROWS)]
    remote(went, went, by_out, by_sem, at(yl_=2 * yy + 1 - yb)).start()
    gathered = b_buf.at[:, pl.ds(own_rows, NROWS)]
    remote(gathered, gathered, bc_out, bc_sem, at(c_=1 - c)).start()

    @pl.when(attends)
    def _():
        await_bytes(kv_peer, kv_sem)
        await_bytes(t_recv, t_sem)
        c2 = SCALE * LOG2E

        def attend(i, carry):
            q = qkv[pl.ds(i * 8, 8), 0].reshape(128, HD)
            s_a = nt_dot(q, qkv[:, 1].reshape(512, HD))
            s_b = nt_dot(q, kv_peer[:, 0].reshape(512, HD))
            peak = jnp.maximum(
                jnp.max(s_a, axis=-1, keepdims=True), jnp.max(s_b, axis=-1, keepdims=True)
            )
            e_a = jnp.exp2((s_a - peak) * c2)
            e_b = jnp.exp2((s_b - peak) * c2)
            total = jnp.sum(e_a, axis=-1, keepdims=True) + jnp.sum(e_b, axis=-1, keepdims=True)
            o = jnp.dot(
                e_a.astype(BF16), qkv[:, 2].reshape(512, HD), preferred_element_type=F32
            ) + jnp.dot(
                e_b.astype(BF16), kv_peer[:, 1].reshape(512, HD), preferred_element_type=F32
            )
            o = o / total + t_recv[pl.ds(i * 8, 8)].astype(F32).reshape(128, HD)
            o_buf[i] = o.astype(BF16).reshape(2, 2, 2, 16, HD)
            for b in range(2):
                for yd in range(4):
                    zd = 2 * i + b
                    here = jnp.logical_and(zd == z, yl == yd)
                    src, dst = o_buf.at[i, :, :, yd % 2], att.at[pair_head, :, :, yl]

                    @pl.when(here)
                    def _(src=src, dst=dst):
                        pltpu.make_async_copy(src, dst, o_sem).start()

                    @pl.when(jnp.logical_not(here))
                    def _(src=src, dst=dst, zd=zd, yd=yd):
                        remote(src, dst, o_out.at[i], o_sem, at(z_=zd, yl_=yd)).start()

            return carry

        lax.fori_loop(0, 4, attend, 0)

    await_bytes(b_buf.at[:, pl.ds(near_rows, ZROWS)], by_sem)
    await_bytes(b_buf.at[:, pl.ds(near_rows, YROWS)], bz_sem)
    gathered_near = b_buf.at[:, pl.ds(near_rows, NROWS)]
    remote(gathered_near, gathered_near, bd_out, bd_sem, at(c_=1 - c)).start()

    await_bytes(att, o_sem)
    tokens = [
        jnp.concatenate([att[h, zz].reshape(128, HD) for h in range(3)], axis=1) for zz in range(2)
    ]
    stacked = jnp.concatenate(tokens, axis=0)
    beside = jnp.concatenate(tokens, axis=1)
    blank = jnp.zeros((64, 384), BF16)
    main_rows = pl.multiple_of(yy * 64, 64)
    tail_rows = pl.multiple_of((1 - yy) * 256, 64)
    mine = yh == half
    early = jnp.where(mine, 1 - yy, yy)
    order = (early, 1 - early)
    await_bytes(b_buf.at[:, pl.ds(own_rows, NROWS)], bc_sem)
    await_bytes(b_buf.at[:, pl.ds(near_rows, NROWS)], bd_sem)

    def project(xd):
        main = nt_dot(stacked, b_buf[xd, pl.ds(main_rows, 256), :]).reshape(2, 2, 64, 256)
        ends = b_buf[xd, pl.ds(tail_rows, 64), :]
        weights = jnp.concatenate(
            [
                jnp.concatenate([ends, blank], axis=1),
                jnp.concatenate([blank, ends], axis=1),
            ],
            axis=0,
        )
        tail = nt_dot(beside, weights).reshape(2, 64, 128)
        return jnp.concatenate([main[0], main[1], tail], axis=-1)

    for n, k in enumerate((2, 1, 3)):
        xd = (x + k) % 4
        cx_send[n] = project(xd).astype(BF16)
        remote(
            cx_send.at[n, order[0]], cx_recv.at[0, n], cx_out, cx_sem.at[0], at(x_=xd)
        ).start()
    for n, k in enumerate((2, 1, 3)):
        remote(
            cx_send.at[n, order[1]], cx_recv.at[1, n], cx_out, cx_sem.at[1], at(x_=(x + k) % 4)
        ).start()
    cx_own[...] = project(x)

    lane_half = lax.broadcasted_iota(jnp.int32, (64, 128), 1) // 64
    for i in range(2):
        await_bytes(cx_recv.at[i], cx_sem.at[i])
        total = cx_own[order[i]]
        for n in range(3):
            total = total + cx_recv[i, n].astype(F32)
        ends = total[:, 512:640]
        turned = pltpu.roll(ends, 64, 1)
        for zz in range(2):
            placed = jnp.where(lane_half == yy, jnp.where(yy == zz, ends, turned), 0.0)
            y_send[i, zz, :, :256] = total[:, zz * 256 : zz * 256 + 256].astype(BF16)
            y_send[i, zz, :, 256:] = placed.astype(BF16)
            src, dst = y_send.at[i, zz], y_out_ref.at[yh, yy]
            here = jnp.logical_and(mine, jnp.logical_and(z % 2 == zz, order[i] == yy))

            @pl.when(here)
            def _(src=src, dst=dst):
                pltpu.make_async_copy(src, dst, y_sem).start()

            @pl.when(jnp.logical_not(here))
            def _(src=src, dst=dst, zz=zz, i=i):
                remote(
                    src, dst, y_out, y_sem, at(z_=base + zz, yl_=2 * order[i] + yb, yh_=half)
                ).start()

    await_bytes(y_out_ref, y_sem)

    @pl.when(mine)
    def _():
        await_bytes(b_buf.at[0, pl.ds(0, 192)], y_out)

    @pl.when(jnp.logical_not(mine))
    def _():
        await_bytes(y_out_ref, y_out)

    @pl.when(attends)
    def _():
        await_bytes(emb.at[pl.ds(0, 11)], qkv_out)
        await_bytes(t_send.at[pl.ds(0, 11)], t_out)
        await_bytes(kv_peer, kv_out)
        for i in range(4):

            @pl.when(z // 2 == i)
            def _(i=i):
                await_bytes(kv_peer.at[pl.ds(0, 14)], o_out.at[i])

            @pl.when(z // 2 != i)
            def _(i=i):
                await_bytes(kv_peer.at[pl.ds(0, 16)], o_out.at[i])

    @pl.when(jnp.logical_not(attends))
    def _():
        await_bytes(emb, qkv_out)
        await_bytes(t_send, t_out)

    @pl.when(z % 2 == first)
    def _():
        await_bytes(b_buf.at[pl.ds(0, 3), pl.ds(0, NROWS)], b_out)
        await_bytes(b_buf.at[pl.ds(0, 3), pl.ds(0, YROWS)], bz_out)

    @pl.when(z % 2 != first)
    def _():
        await_bytes(b_buf.at[:, pl.ds(0, NROWS)], b_out)
        await_bytes(b_buf.at[:, pl.ds(0, YROWS)], bz_out)

    await_bytes(near, near_out)
    await_bytes(b_buf.at[:, pl.ds(0, ZROWS)], by_out)
    await_bytes(b_buf.at[:, pl.ds(0, NROWS)], bc_out)
    await_bytes(b_buf.at[:, pl.ds(0, NROWS)], bd_out)
    await_bytes(cx_send, cx_out)


def shards(fresh, still_masked, actions, action_table, mask_vector, position, cache, w_out):
    anywhere = pl.BlockSpec(memory_space=pl.ANY)
    vmem = pl.BlockSpec(memory_space=pltpu.VMEM)
    smem = pl.BlockSpec(memory_space=pltpu.SMEM)
    dma = pltpu.SemaphoreType.DMA
    parts = pl.pallas_call(
        kernel,
        out_shape=jax.ShapeDtypeStruct((2, 2, 64, 384), BF16),
        in_specs=[smem, vmem, vmem, vmem, anywhere, anywhere, anywhere, anywhere],
        out_specs=anywhere,
        scratch_shapes=[
            pltpu.VMEM((3, 4, 16, 384), BF16),
            pltpu.VMEM((3, 16, 384), BF16),
            pltpu.VMEM((2, 16, 4, 16, 384), BF16),
            pltpu.VMEM((NROWS, 384), BF16),
            pltpu.VMEM((12, 3, 16, HD), BF16),
            pltpu.VMEM((32, 3, 16, HD), BF16),
            pltpu.VMEM((32, 2, 16, HD), BF16),
            pltpu.VMEM((12, 16, HD), BF16),
            pltpu.VMEM((32, 16, HD), BF16),
            pltpu.VMEM((4, 2, 2, 2, 16, HD), BF16),
            pltpu.VMEM((3, 2, 2, 4, 16, HD), BF16),
            pltpu.VMEM((YROWS, 384), BF16),
            pltpu.VMEM((4, 4 * NROWS, 384), BF16),
            pltpu.VMEM((3, 2, 64, 640), BF16),
            pltpu.VMEM((2, 64, 640), F32),
            pltpu.VMEM((2, 3, 64, 640), BF16),
            pltpu.VMEM((2, 2, 64, 384), BF16),
            dma((4,)),
            dma((4,)),
            dma((2,)),
        ]
        + [dma] * 22,
        compiler_params=pltpu.CompilerParams(
            collective_id=0, has_side_effects=True, vmem_limit_bytes=60 << 20
        ),
        cost_estimate=pl.CostEstimate(
            flops=400_000_000, bytes_accessed=2_000_000, transcendentals=600_000
        ),
    )(
        actions,
        still_masked,
        jnp.transpose(action_table, (1, 0, 2)),
        mask_vector,
        fresh,
        position,
        cache,
        jnp.transpose(w_out),
    )
    parts = parts[0].astype(F32) + parts[1].astype(F32)
    middle = parts[0, :, 256:] + parts[1, :, 256:]
    return jnp.concatenate([parts[0, :, :256], middle, parts[1, :, :256]], axis=1).reshape(
        4, 16, 640
    )


def solution(mesh):
    placed = (
        P(None, None, "patch", "head"),
        P(None, "patch"),
        P(),
        P(None, None, "head"),
        P(None, "head"),
        P(None, "patch", "head"),
        P(None, None, None, "patch", "head"),
        P("head", "patch"),
    )
    return jax.shard_map(
        shards, mesh=mesh, in_specs=placed, out_specs=P(None, "patch", "head"), check_vma=False
    )
```

time: 75.1 us -> 58 us (0.77)
  Pallas kernels: 67.4 us -> 56.1 us
  local copies, waits for them, and re-layouts: 7.32 us -> 0.01 us
  other arithmetic: 0 us -> 1.65 us
    pallas_call x1, Pallas kernels: 67.4 us -> 56.1 us  [shards(): pl.pallas_call(kernel, out_shape=jax.ShapeDtypeStruct((2, 2, 64, 384), BF...]
    unnamed x17 -> x0, local copies, waits for them, and re-layouts: 7.32 us -> none
    add x0 -> x2, other arithmetic: none -> 0.97 us  [the longest x1 0.96 us: shards(): parts = parts[0].astype(F32) + parts[1].astype(F32)]
where the time goes in v2:
time: 58 us; the launch traced here: 57.8 us
  Pallas kernels  56.1 us (97%)
  other arithmetic  1.65 us (3%)
    pallas_call x1, Pallas kernels, shards(): pl.pallas_call(kernel, out_shape=jax.ShapeDtypeStruct((2, 2, 64, 384), BF...  56.1 us

profile of v2, /device:TPU:8, one launch (start us, length us, event | category | flops | bytes accessed | tf_op | source)
XLA Modules:
  0.0 57.8 jit_solution(5172035605607974310)
XLA Ops:
  0.0 56.1 %shard_map.82 = bf16[2,2,64,384]{3,2,1,0:T(8,128)(2,1)} custom-call(s32[4]{0:T(128)} %actions.1, s32[4,16]{1,0:T(4,128)} %still_ref.1, bf16[3,8,384]{2,1,0:T(8,128)(2,1)} %bitcast.11, bf16[3,384]{1,0:T(4,128)(2,1)} %maskv_ref.1, bf16[3,4,16,384]{3,2,1,0:T(8,128)(2,1)} %fresh_hbm.1, bf16[3,16,384]{2,1,0:T(8,128)(2,1)} %pos_hbm.1, ...), custom_call_target="tpu_custom_call" | custom-call | flops 400000000 | bytes 2000000 | tf_op jit(solution)/shard_map/pallas_call | solution.py:359
  56.1 1.0 %add_bitcast_fusion = f32[2,64,384]{2,1,0:T(8,128)S(1)} fusion(bf16[2,2,64,384]{3,2,1,0:T(8,128)(2,1)} %shard_map.82), kind=kLoop, calls=%fused_computation | loop fusion | flops 147456 | bytes 393216 | tf_op jit(solution)/shard_map/add | solution.py:403
  57.1 0.7 %pad_maximum_fusion = f32[4,16,640]{2,1,0:T(8,128)} fusion(f32[4,16,256]{2,1,0:T(8,128)S(1)} %bitcast.8, f32[4,16,128]{2,1,0:T(8,128)S(1)} %bitcast.9, f32[4,16,256]{2,1,0:T(8,128)S(1)} %bitcast.7), kind=kLoop, calls=%fused_computation.1 | loop fusion | flops 81920 | bytes 327680 | tf_op jit(solution)/shard_map/concatenate | solution.py:405
  (2 shorter events, 0.0 us)

commit v3 on v2

--- a/solution.py
+++ b/solution.py
@@ -14,6 +14,7 @@
 SCALE = HD ** (-0.5)
 LOG2E = 1.4426950408889634
 PLACE = (0, 3, 5)
+YPLACE = (0, 1, 2, 3)
 ZROWS, YROWS = 32, 48
 NROWS = ZROWS + YROWS
 
@@ -28,7 +29,7 @@
     actions, still_ref, table_ref, maskv_ref, fresh_hbm, pos_hbm, cache_hbm, w_hbm, y_out_ref,
     fresh, pos, cache, w_own, emb, qkv, kv_peer, t_send, t_recv, o_buf, att, near, b_buf,
     cx_send, cx_own, cx_recv, y_send,
-    in_sem, o_out, cx_sem, qkv_sem, kv_sem, o_sem, t_sem, near_sem, b_sem, bz_sem, by_sem,
+    in_sem, o_out, cx_sem, o_sem, qkv_sem, kv_sem, t_sem, near_sem, b_sem, bz_sem, by_sem,
     bc_sem, bd_sem, y_sem,
     qkv_out, kv_out, t_out, near_out, b_out, bz_out, by_out, bc_out, bd_out, cx_out, y_out,
 ):
@@ -105,13 +106,17 @@
 
     me = z * 4 + yl
     pair_head = jnp.int32(-1)
-    for h in range(3):
-        pair_head = jnp.where((2 * yl + PLACE[h]) % 8 == z, h, pair_head)
+    pair_roll = jnp.int32(0)
+    for r in range(ROLL):
+        for h in range(3):
+            there = jnp.logical_and((2 * r + PLACE[h]) % 8 == z, yl == YPLACE[r])
+            pair_head = jnp.where(there, h, pair_head)
+            pair_roll = jnp.where(there, r, pair_roll)
     attends = pair_head >= 0
 
     def to_attending(src, dst, send, recv, r, h):
         zd = (2 * r + PLACE[h]) % 8
-        here = jnp.logical_and(z == zd, yl == r)
+        here = jnp.logical_and(z == zd, yl == YPLACE[r])
 
         @pl.when(here)
         def _():
@@ -119,9 +124,9 @@
 
         @pl.when(jnp.logical_not(here))
         def _():
-            remote(src, dst, send, recv, at(z_=zd, yl_=r)).start()
-
-    for r in range(ROLL):
+            remote(src, dst, send, recv, at(z_=zd, yl_=YPLACE[r])).start()
+
+    for r in (0, 1, 2, 3):
         for h in range(3):
             to_attending(emb.at[r * 3 + h], qkv.at[me], qkv_out, qkv_sem, r, h)
 
@@ -220,15 +225,17 @@
                 for yd in range(4):
                     zd = 2 * i + b
                     here = jnp.logical_and(zd == z, yl == yd)
-                    src, dst = o_buf.at[i, :, :, yd % 2], att.at[pair_head, :, :, yl]
+                    src, dst = o_buf.at[i, :, :, yd % 2], att.at[pair_head, :, :, pair_roll]
 
                     @pl.when(here)
                     def _(src=src, dst=dst):
-                        pltpu.make_async_copy(src, dst, o_sem).start()
+                        pltpu.make_async_copy(src, dst, o_sem.at[pair_roll // 2]).start()
 
                     @pl.when(jnp.logical_not(here))
                     def _(src=src, dst=dst, zd=zd, yd=yd):
-                        remote(src, dst, o_out.at[i], o_sem, at(z_=zd, yl_=yd)).start()
+                        remote(
+                            src, dst, o_out.at[i], o_sem.at[pair_roll // 2], at(z_=zd, yl_=yd)
+                        ).start()
 
             return carry
 
@@ -239,70 +246,81 @@
     gathered_near = b_buf.at[:, pl.ds(near_rows, NROWS)]
     remote(gathered_near, gathered_near, bd_out, bd_sem, at(c_=1 - c)).start()
 
-    await_bytes(att, o_sem)
-    tokens = [
-        jnp.concatenate([att[h, zz].reshape(128, HD) for h in range(3)], axis=1) for zz in range(2)
-    ]
-    stacked = jnp.concatenate(tokens, axis=0)
-    beside = jnp.concatenate(tokens, axis=1)
+    await_bytes(b_buf.at[:, pl.ds(own_rows, NROWS)], bc_sem)
+    await_bytes(b_buf.at[:, pl.ds(near_rows, NROWS)], bd_sem)
     blank = jnp.zeros((64, 384), BF16)
     main_rows = pl.multiple_of(yy * 64, 64)
     tail_rows = pl.multiple_of((1 - yy) * 256, 64)
     mine = yh == half
     early = jnp.where(mine, 1 - yy, yy)
     order = (early, 1 - early)
-    await_bytes(b_buf.at[:, pl.ds(own_rows, NROWS)], bc_sem)
-    await_bytes(b_buf.at[:, pl.ds(near_rows, NROWS)], bd_sem)
-
-    def project(xd):
-        main = nt_dot(stacked, b_buf[xd, pl.ds(main_rows, 256), :]).reshape(2, 2, 64, 256)
-        ends = b_buf[xd, pl.ds(tail_rows, 64), :]
-        weights = jnp.concatenate(
-            [
-                jnp.concatenate([ends, blank], axis=1),
-                jnp.concatenate([blank, ends], axis=1),
-            ],
-            axis=0,
-        )
-        tail = nt_dot(beside, weights).reshape(2, 64, 128)
-        return jnp.concatenate([main[0], main[1], tail], axis=-1)
-
-    for n, k in enumerate((2, 1, 3)):
-        xd = (x + k) % 4
-        cx_send[n] = project(xd).astype(BF16)
-        remote(
-            cx_send.at[n, order[0]], cx_recv.at[0, n], cx_out, cx_sem.at[0], at(x_=xd)
-        ).start()
-    for n, k in enumerate((2, 1, 3)):
-        remote(
-            cx_send.at[n, order[1]], cx_recv.at[1, n], cx_out, cx_sem.at[1], at(x_=(x + k) % 4)
-        ).start()
-    cx_own[...] = project(x)
-
-    lane_half = lax.broadcasted_iota(jnp.int32, (64, 128), 1) // 64
-    for i in range(2):
-        await_bytes(cx_recv.at[i], cx_sem.at[i])
-        total = cx_own[order[i]]
-        for n in range(3):
-            total = total + cx_recv[i, n].astype(F32)
-        ends = total[:, 512:640]
-        turned = pltpu.roll(ends, 64, 1)
-        for zz in range(2):
-            placed = jnp.where(lane_half == yy, jnp.where(yy == zz, ends, turned), 0.0)
-            y_send[i, zz, :, :256] = total[:, zz * 256 : zz * 256 + 256].astype(BF16)
-            y_send[i, zz, :, 256:] = placed.astype(BF16)
-            src, dst = y_send.at[i, zz], y_out_ref.at[yh, yy]
-            here = jnp.logical_and(mine, jnp.logical_and(z % 2 == zz, order[i] == yy))
-
-            @pl.when(here)
-            def _(src=src, dst=dst):
-                pltpu.make_async_copy(src, dst, y_sem).start()
-
-            @pl.when(jnp.logical_not(here))
-            def _(src=src, dst=dst, zz=zz, i=i):
-                remote(
-                    src, dst, y_out, y_sem, at(z_=base + zz, yl_=2 * order[i] + yb, yh_=half)
-                ).start()
+    spans = [pl.ds(pl.multiple_of(order[i] * 32, 32), 32) for i in range(2)]
+
+    for w in range(2):
+        await_bytes(att.at[:, :, :, pl.ds(2 * w, 2)], o_sem.at[w])
+        tokens = [
+            jnp.concatenate(
+                [att[h, zz, :, 2 * w : 2 * w + 2].reshape(64, HD) for h in range(3)], axis=1
+            )
+            for zz in range(2)
+        ]
+        stacked = jnp.concatenate(tokens, axis=0)
+        beside = jnp.concatenate(tokens, axis=1)
+
+        def project(xd, stacked=stacked, beside=beside):
+            main = nt_dot(stacked, b_buf[xd, pl.ds(main_rows, 256), :])
+            ends = b_buf[xd, pl.ds(tail_rows, 64), :]
+            weights = jnp.concatenate(
+                [
+                    jnp.concatenate([ends, blank], axis=1),
+                    jnp.concatenate([blank, ends], axis=1),
+                ],
+                axis=0,
+            )
+            return jnp.concatenate([main[:64], main[64:], nt_dot(beside, weights)], axis=1)
+
+        def to_x(i, n, k, w=w):
+            remote(
+                cx_send.at[w, n, spans[i]], cx_recv.at[w, i, n], cx_out, cx_sem.at[2 * w + i],
+                at(x_=(x + k) % 4),
+            ).start()
+
+        for n, k in enumerate((2, 1, 3)):
+            cx_send[w, n] = project((x + k) % 4).astype(BF16)
+            to_x(0, n, k)
+        for n, k in enumerate((2, 1, 3)):
+            to_x(1, n, k)
+        cx_own[w] = project(x)
+
+    lane_half = lax.broadcasted_iota(jnp.int32, (32, 128), 1) // 64
+    main_lanes = pl.multiple_of(yy * 128, 128)
+    tail_lanes = pl.multiple_of((1 - yy) * 256, 128)
+    for w in range(2):
+        for i in range(2):
+            await_bytes(cx_recv.at[w, i], cx_sem.at[2 * w + i])
+            total = cx_own[w, spans[i]]
+            for n in range(3):
+                total = total + cx_recv[w, i, n].astype(F32)
+            ends = total[:, 512:640]
+            turned = pltpu.roll(ends, 64, 1)
+            for zz in range(2):
+                placed = jnp.where(lane_half == yy, jnp.where(yy == zz, ends, turned), 0.0)
+                y_send[w, i, zz, :, pl.ds(main_lanes, 256)] = total[
+                    :, zz * 256 : zz * 256 + 256
+                ].astype(BF16)
+                y_send[w, i, zz, :, pl.ds(tail_lanes, 128)] = placed.astype(BF16)
+                src, dst = y_send.at[w, i, zz], y_out_ref.at[yh, yy, w]
+                here = jnp.logical_and(mine, jnp.logical_and(z % 2 == zz, order[i] == yy))
+
+                @pl.when(here)
+                def _(src=src, dst=dst):
+                    pltpu.make_async_copy(src, dst, y_sem).start()
+
+                @pl.when(jnp.logical_not(here))
+                def _(src=src, dst=dst, zz=zz, i=i):
+                    remote(
+                        src, dst, y_out, y_sem, at(z_=base + zz, yl_=2 * order[i] + yb, yh_=half)
+                    ).start()
 
     await_bytes(y_out_ref, y_sem)
 
@@ -358,7 +376,7 @@
     dma = pltpu.SemaphoreType.DMA
     parts = pl.pallas_call(
         kernel,
-        out_shape=jax.ShapeDtypeStruct((2, 2, 64, 384), BF16),
+        out_shape=jax.ShapeDtypeStruct((2, 2, 2, 32, 384), BF16),
         in_specs=[smem, vmem, vmem, vmem, anywhere, anywhere, anywhere, anywhere],
         out_specs=anywhere,
         scratch_shapes=[
@@ -375,15 +393,16 @@
             pltpu.VMEM((3, 2, 2, 4, 16, HD), BF16),
             pltpu.VMEM((YROWS, 384), BF16),
             pltpu.VMEM((4, 4 * NROWS, 384), BF16),
-            pltpu.VMEM((3, 2, 64, 640), BF16),
+            pltpu.VMEM((2, 3, 64, 640), BF16),
             pltpu.VMEM((2, 64, 640), F32),
-            pltpu.VMEM((2, 3, 64, 640), BF16),
-            pltpu.VMEM((2, 2, 64, 384), BF16),
+            pltpu.VMEM((2, 2, 3, 32, 640), BF16),
+            pltpu.VMEM((2, 2, 2, 32, 384), BF16),
+            dma((4,)),
             dma((4,)),
             dma((4,)),
             dma((2,)),
         ]
-        + [dma] * 22,
+        + [dma] * 21,
         compiler_params=pltpu.CompilerParams(
             collective_id=0, has_side_effects=True, vmem_limit_bytes=60 << 20
         ),
@@ -400,11 +419,12 @@
         cache,
         jnp.transpose(w_out),
     )
-    parts = parts[0].astype(F32) + parts[1].astype(F32)
-    middle = parts[0, :, 256:] + parts[1, :, 256:]
-    return jnp.concatenate([parts[0, :, :256], middle, parts[1, :, :256]], axis=1).reshape(
-        4, 16, 640
-    )
+    parts = parts.reshape(2, 2, 64, 384)
+    return sum(
+        jnp.pad(parts[k, b].astype(F32), ((0, 0), (256 * b, 256 * (1 - b))))
+        for k in range(2)
+        for b in range(2)
+    ).reshape(4, 16, 640)
 
 
 def solution(mesh):

time: 58 us -> 57.2 us (0.986)
  other arithmetic: 1.65 us -> 0.69 us
  local copies, waits for them, and re-layouts: 0.01 us -> 0.89 us
  Pallas kernels: 56.1 us -> 55.3 us
    convert_element_type x0 -> x1, local copies, waits for them, and re-layouts: none -> 0.89 us  [shards(): parts[k, b].astype(F32)]
    pallas_call x1, Pallas kernels: 56.1 us -> 55.3 us  [shards(): pl.pallas_call(kernel, out_shape=jax.ShapeDtypeStruct((2, 2, 2, 32, 384),...]
    concatenate x1 -> x0, other arithmetic: 0.68 us -> none  [shards(): jnp.concatenate([parts[0, :, :256], middle, parts[1, :, :256]], axis=1)]
where the time goes in v3:
time: 57.2 us; the launch traced here: 56.9 us
  Pallas kernels  55.3 us (97%)
  local copies, waits for them, and re-layouts  0.89 us (2%)
  other arithmetic  0.69 us (1%)
    pallas_call x1, Pallas kernels, shards(): pl.pallas_call(kernel, out_shape=jax.ShapeDtypeStruct((2, 2, 2, 32, 384),...  55.3 us

profile of v3, /device:TPU:8, one launch (start us, length us, event | category | flops | bytes accessed | tf_op | source)
XLA Modules:
  0.0 56.9 jit_solution(6593234473319483627)
XLA Ops:
  0.0 55.3 %shard_map.82 = bf16[2,2,2,32,384]{4,3,2,1,0:T(8,128)(2,1)} custom-call(s32[4]{0:T(128)} %actions.1, s32[4,16]{1,0:T(4,128)} %still_ref.1, bf16[3,8,384]{2,1,0:T(8,128)(2,1)} %bitcast.14, bf16[3,384]{1,0:T(4,128)(2,1)} %maskv_ref.1, bf16[3,4,16,384]{3,2,1,0:T(8,128)(2,1)} %fresh_hbm.1, bf16[3,16,384]{2,1,0:T(8,128)(2,1)} %pos_hbm.1, ...), custom_call_target="tpu_custom_call" | custom-call | flops 400000000 | bytes 2000000 | tf_op jit(solution)/shard_map/pallas_call | solution.py:377
  55.3 0.9 %slice_bitcast_fusion.3 = (bf16[64,384]{1,0:T(8,128)(2,1)S(1)}, bf16[64,384]{1,0:T(8,128)(2,1)S(1)}, bf16[64,384]{1,0:T(8,128)(2,1)S(1)}, bf16[64,384]{1,0:T(8,128)(2,1)S(1)}) fusion(bf16[2,2,64,384]{3,2,1,0:T(8,128)(2,1)} %bitcast.12), kind=kLoop, calls=%fused_computation.4 | loop fusion | bytes 393216 | tf_op jit(solution)/shard_map/convert_element_type | solution.py:424
  56.2 0.7 %convert_add_fusion = f32[64,640]{1,0:T(8,128)} fusion(bf16[64,384]{1,0:T(8,128)(2,1)S(1)} %get-tuple-element.6, bf16[64,384]{1,0:T(8,128)(2,1)S(1)} %get-tuple-element.7, bf16[64,384]{1,0:T(8,128)(2,1)S(1)} %get-tuple-element.8, bf16[64,384]{1,0:T(8,128)(2,1)S(1)} %get-tuple-element.5), kind=kLoop, calls=%fused_computation | loop fusion | flops 286720 | bytes 360448 | tf_op jit(solution)/shard_map/add | solution.py:423

commit v4 on v3

--- a/solution.py
+++ b/solution.py
@@ -74,7 +74,8 @@
         hail(at(z_=s // 4, yl_=s % 4))
         return carry
 
-    lax.fori_loop(1, 32, hail_group, 0)
+    for i in (16, 15, 17, 14, 18, 13, 19, 12, 20, 11, 21, 10, 22, 9, 23, 8, 24, 7, 25, 6, 26, 5, 27, 4, 28, 3, 29, 2, 30, 1, 31):
+        hail_group(i, 0)
     hail(at(c_=1 - c))
     for k in (1, 2, 3):
         hail(at(x_=(x + k) % 4))
@@ -222,10 +223,11 @@
             o = o / total + t_recv[pl.ds(i * 8, 8)].astype(F32).reshape(128, HD)
             o_buf[i] = o.astype(BF16).reshape(2, 2, 2, 16, HD)
             for b in range(2):
-                for yd in range(4):
+                for step in (2, 1, 3, 0):
+                    yd = (yl + step) % 4
                     zd = 2 * i + b
                     here = jnp.logical_and(zd == z, yl == yd)
-                    src, dst = o_buf.at[i, :, :, yd % 2], att.at[pair_head, :, :, pair_roll]
+                    src, dst = o_buf.at[i, :, :, (yl + step) % 2], att.at[pair_head, :, :, pair_roll]
 
                     @pl.when(here)
                     def _(src=src, dst=dst):
@@ -285,10 +287,10 @@
                 at(x_=(x + k) % 4),
             ).start()
 
-        for n, k in enumerate((2, 1, 3)):
+        for n, k in enumerate((2, 3, 1)):
             cx_send[w, n] = project((x + k) % 4).astype(BF16)
             to_x(0, n, k)
-        for n, k in enumerate((2, 1, 3)):
+        for n, k in enumerate((2, 3, 1)):
             to_x(1, n, k)
         cx_own[w] = project(x)
 

time: 57.2 us -> 56.8 us (level)
  no operation moved by 1% of the time
where the time goes in v4:
time: 56.8 us; the launch traced here: 56.5 us
  Pallas kernels  54.9 us (97%)
  local copies, waits for them, and re-layouts  0.89 us (2%)
  other arithmetic  0.69 us (1%)
    pallas_call x1, Pallas kernels, shards(): pl.pallas_call(kernel, out_shape=jax.ShapeDtypeStruct((2, 2, 2, 32, 384),...  54.9 us

profile of v4, /device:TPU:8, one launch (start us, length us, event | category | flops | bytes accessed | tf_op | source)
XLA Modules:
  0.0 56.5 jit_solution(1558686842616498092)
XLA Ops:
  0.0 54.9 %shard_map.82 = bf16[2,2,2,32,384]{4,3,2,1,0:T(8,128)(2,1)} custom-call(s32[4]{0:T(128)} %actions.1, s32[4,16]{1,0:T(4,128)} %still_ref.1, bf16[3,8,384]{2,1,0:T(8,128)(2,1)} %bitcast.14, bf16[3,384]{1,0:T(4,128)(2,1)} %maskv_ref.1, bf16[3,4,16,384]{3,2,1,0:T(8,128)(2,1)} %fresh_hbm.1, bf16[3,16,384]{2,1,0:T(8,128)(2,1)} %pos_hbm.1, ...), custom_call_target="tpu_custom_call" | custom-call | flops 400000000 | bytes 2000000 | tf_op jit(solution)/shard_map/pallas_call | solution.py:379
  54.9 0.9 %slice_bitcast_fusion.3 = (bf16[64,384]{1,0:T(8,128)(2,1)S(1)}, bf16[64,384]{1,0:T(8,128)(2,1)S(1)}, bf16[64,384]{1,0:T(8,128)(2,1)S(1)}, bf16[64,384]{1,0:T(8,128)(2,1)S(1)}) fusion(bf16[2,2,64,384]{3,2,1,0:T(8,128)(2,1)} %bitcast.12), kind=kLoop, calls=%fused_computation.4 | loop fusion | bytes 393216 | tf_op jit(solution)/shard_map/convert_element_type | solution.py:426
  55.8 0.7 %convert_add_fusion = f32[64,640]{1,0:T(8,128)} fusion(bf16[64,384]{1,0:T(8,128)(2,1)S(1)} %get-tuple-element.6, bf16[64,384]{1,0:T(8,128)(2,1)S(1)} %get-tuple-element.7, bf16[64,384]{1,0:T(8,128)(2,1)S(1)} %get-tuple-element.8, bf16[64,384]{1,0:T(8,128)(2,1)S(1)} %get-tuple-element.5), kind=kLoop, calls=%fused_computation | loop fusion | flops 286720 | bytes 360448 | tf_op jit(solution)/shard_map/add | solution.py:425

commit v5 on v4

--- a/solution.py
+++ b/solution.py
@@ -13,7 +13,7 @@
 FRAMES = 16
 SCALE = HD ** (-0.5)
 LOG2E = 1.4426950408889634
-PLACE = (0, 3, 5)
+PLACE = ((0, 3, 5), (2, 5, 7), (1, 4, 6), (0, 3, 6))
 YPLACE = (0, 1, 2, 3)
 ZROWS, YROWS = 32, 48
 NROWS = ZROWS + YROWS
@@ -110,13 +110,13 @@
     pair_roll = jnp.int32(0)
     for r in range(ROLL):
         for h in range(3):
-            there = jnp.logical_and((2 * r + PLACE[h]) % 8 == z, yl == YPLACE[r])
+            there = jnp.logical_and(PLACE[r][h] == z, yl == YPLACE[r])
             pair_head = jnp.where(there, h, pair_head)
             pair_roll = jnp.where(there, r, pair_roll)
     attends = pair_head >= 0
 
     def to_attending(src, dst, send, recv, r, h):
-        zd = (2 * r + PLACE[h]) % 8
+        zd = PLACE[r][h]
         here = jnp.logical_and(z == zd, yl == YPLACE[r])
 
         @pl.when(here)

time: 56.8 us -> 56.6 us (level)
  the two profiles are of different devices: /device:TPU:8 before, /device:TPU:392 now
where the time goes in v5:
time: 56.6 us; the launch traced here: 56.4 us
  Pallas kernels  54.8 us (97%)
  local copies, waits for them, and re-layouts  0.89 us (2%)
  other arithmetic  0.69 us (1%)
    pallas_call x1, Pallas kernels, shards(): pl.pallas_call(kernel, out_shape=jax.ShapeDtypeStruct((2, 2, 2, 32, 384),...  54.8 us

profile of v5, /device:TPU:392, one launch (start us, length us, event | category | flops | bytes accessed | tf_op | source)
XLA Modules:
  0.0 56.4 jit_solution(8797151724069661808)
XLA Ops:
  0.0 54.8 %shard_map.82 = bf16[2,2,2,32,384]{4,3,2,1,0:T(8,128)(2,1)} custom-call(s32[4]{0:T(128)} %actions.1, s32[4,16]{1,0:T(4,128)} %still_ref.1, bf16[3,8,384]{2,1,0:T(8,128)(2,1)} %bitcast.14, bf16[3,384]{1,0:T(4,128)(2,1)} %maskv_ref.1, bf16[3,4,16,384]{3,2,1,0:T(8,128)(2,1)} %fresh_hbm.1, bf16[3,16,384]{2,1,0:T(8,128)(2,1)} %pos_hbm.1, ...), custom_call_target="tpu_custom_call" | custom-call | flops 400000000 | bytes 2000000 | tf_op jit(solution)/shard_map/pallas_call | solution.py:379
  54.8 0.9 %slice_bitcast_fusion.3 = (bf16[64,384]{1,0:T(8,128)(2,1)S(1)}, bf16[64,384]{1,0:T(8,128)(2,1)S(1)}, bf16[64,384]{1,0:T(8,128)(2,1)S(1)}, bf16[64,384]{1,0:T(8,128)(2,1)S(1)}) fusion(bf16[2,2,64,384]{3,2,1,0:T(8,128)(2,1)} %bitcast.12), kind=kLoop, calls=%fused_computation.4 | loop fusion | bytes 393216 | tf_op jit(solution)/shard_map/convert_element_type | solution.py:426
  55.7 0.7 %convert_add_fusion = f32[64,640]{1,0:T(8,128)} fusion(bf16[64,384]{1,0:T(8,128)(2,1)S(1)} %get-tuple-element.6, bf16[64,384]{1,0:T(8,128)(2,1)S(1)} %get-tuple-element.7, bf16[64,384]{1,0:T(8,128)(2,1)S(1)} %get-tuple-element.8, bf16[64,384]{1,0:T(8,128)(2,1)S(1)} %get-tuple-element.5), kind=kLoop, calls=%fused_computation | loop fusion | flops 286720 | bytes 360448 | tf_op jit(solution)/shard_map/add | solution.py:425
